TPU v7x, 32 devices: a whole 2x2x4 slice. The times are simulated.
32 devices in a mesh: blk: 4 (over y, core), rep: 8 (over z, x).
Axes of the slice: x: 2, y: 2, z: 4, core: 2. Of those that a mesh axis runs over, the one named last changes fastest.
Arguments:
- grad_out: bfloat16 [4096, 256], P(('blk', 'rep')), may hold values from -6 to 6
- relu_bits: int32 [4096, 256], P(('blk', 'rep')), may hold values 0 or 1
- features: bfloat16 [4096, 256], P(('blk', 'rep')), may hold values from -6 to 6
- weight: bfloat16 [256, 256], replicated, may hold values from -0.375 to 0.375
- tiles: bfloat16 [32, 4, 2, 128, 128], P(('blk', 'rep')), as said below
- tile_rows: int32 [32, 4, 2], P(('blk', 'rep')), may hold values from 0 to 7
- tile_counts: int32 [32, 4], P(('blk', 'rep')), may hold values from 1 to 2, as said below
Outputs:
- grad_features: bfloat16 [4096, 256], P(('blk', 'rep'))
- grad_weight: float32 [256, 256], replicated
Inputs may be any that keep to these rules, and one draw needn't show every extreme that they name: `tile_counts`: for every sub-block, some source block has exactly 2 nonzero tiles; loads differ between sub-blocks. `tiles`: about one entry in eight of a tile is nonzero.
All inputs are finite; a program needn't handle non-finite values. No bound on the sum of `relu_bits` on one device may be relied on, other than what follows from the above.
Results may differ from a plain program's by a relative error of at most 0.005.
Values may be sent and summed in bfloat16 or wider, within the bound.
A program may use at most 64 MiB of HBM per device.

v0:
```python
import jax
import jax.numpy as jnp
from jax import lax
from jax.sharding import PartitionSpec as P


def from_behind(array, axis, by):
    devices = lax.axis_size(axis)
    return lax.ppermute(array, axis, [(i, (i + by) % devices) for i in range(devices)])


def body(grad_out, relu_bits, features, weight, tiles, tile_rows, tile_counts):
    nblk = lax.axis_size("blk")
    nrep = lax.axis_size("rep")
    my_block = lax.axis_index("blk")
    rows_here = grad_out.shape[0]
    width = grad_out.shape[1]
    tile_height = tiles.shape[4]
    slot_count = tiles.shape[2]
    block_tiles = rows_here * nrep // tile_height
    masked = jnp.where(relu_bits == 1, grad_out, jnp.zeros_like(grad_out))
    slots = jnp.arange(slot_count, dtype=jnp.int32)
    my_tiles = tiles[0]
    my_rows = tile_rows[0]
    my_counts = tile_counts[0]

    def accumulate(partial_value, piece, source):
        tile_set = lax.dynamic_index_in_dim(my_tiles, source, 0, keepdims=False)
        rows_set = lax.dynamic_index_in_dim(my_rows, source, 0, keepdims=False)
        count = lax.dynamic_index_in_dim(my_counts, source, 0, keepdims=False)
        prods = jnp.einsum("krt,rf->ktf", tile_set, piece, preferred_element_type=jnp.float32)
        live = (slots < count)[:, None, None]
        prods = jnp.where(live, prods, jnp.zeros_like(prods))
        return partial_value.at[rows_set].add(prods)

    partial_value = jnp.zeros((block_tiles, tile_height, width), jnp.float32)
    partial_value = accumulate(partial_value, masked, my_block)

    def one_turn(turn, carry):
        partial_value, held = carry
        held = from_behind(held, "blk", 1)
        source = (my_block - turn) % nblk
        return (accumulate(partial_value, held, source), held)

    partial_value, held = lax.fori_loop(1, nblk, one_turn, (partial_value, masked))
    summed = lax.psum_scatter(
        partial_value.reshape(block_tiles * tile_height, width),
        "rep",
        scatter_dimension=0,
        tiled=True,
    )
    aggregated = summed.astype(jnp.bfloat16)
    grad_features = lax.dot_general(
        aggregated, weight, (((1,), (1,)), ((), ())), preferred_element_type=jnp.float32
    ).astype(jnp.bfloat16)
    weight_term = lax.dot_general(
        features, aggregated, (((0,), (0,)), ((), ())), preferred_element_type=jnp.float32
    )
    total_nodes = rows_here * nrep * nblk
    grad_weight = lax.psum(weight_term, ("blk", "rep")) * total_nodes ** (-0.5)
    return (grad_features, grad_weight)


def solution(mesh):
    return jax.shard_map(
        body,
        mesh=mesh,
        in_specs=(
            P(("blk", "rep"), None),
            P(("blk", "rep"), None),
            P(("blk", "rep"), None),
            P(),
            P(("blk", "rep"), None, None, None, None),
            P(("blk", "rep"), None, None),
            P(("blk", "rep"), None),
        ),
        out_specs=(P(("blk", "rep"), None), P()),
        check_vma=False,
    )
```

profile of v0, /device:TPU:0, one launch (start us, length us, event | category | flops | bytes accessed | tf_op | source)
XLA Modules:
  0.0 233.4 jit_solution(499865236234513302)
XLA Ops:
  7.2 0.0 copy-start
  7.2 0.0 reduce-scatter.2.cloned.1.call-start
  7.2 0.0 copy-start.7
  7.2 0.7 copy-done.7
  7.9 0.6 constant_dynamic-slice_fusion
  8.5 0.0 copy-start.6
  8.5 0.7 iota_compare_fusion.1
  9.2 0.0 copy-done.6
  9.2 0.2 dynamic-slice_reduce_fusion
  9.4 0.1 copy.11
  9.5 0.0 copy-start.3
  9.5 0.0 copy-start.5
  9.5 1.2 copy.10
  10.7 0.0 copy-done.3
  10.7 0.0 copy-done.5
  10.7 1.0 convolution_select_fusion.1
  11.8 0.1 broadcast_in_dim.41
  11.8 0.7 scatter_fusion.1
  12.5 14.6 %while.18 = (s32[]{:T(128)}, f32[8,128,256]{2,1,0:T(8,128)S(1)}, bf16[128,256]{1,0:T(8,128)(2,1)S(1)}, s32[]{:T(128)}, s32[4,2]{1,0:T(4,128)S(1)}, /*index=5*/s3...) while((s32[]{:T(128)}, f32[8,128,256]{2,1,0:T(8,128)S(1)}, ...), condition=%wide.region_3.4_spmd.clone, body=%wide.region_1.3_spmd.clone.sunk | while | flops 16908312 | bytes 1573730 | solution.py:45
  12.6 0.5 collective-permute-start
  13.1 0.6 dynamic_slice.64
  13.7 0.6 iota_compare_fusion.3
  14.3 2.6 %collective-permute-done = bf16[128,256]{1,0:T(8,128)(2,1)S(1)} collective-permute-done((bf16[128,256]{1,0:T(8,128)(2,1)S(1)}, bf16[128,256]{1,0:T(8,128)(2,1)S(1)}, u32[]{:S(2)}, u32[]{:S(2)}) %collective-permute-start) | collective-permute-done | bytes 65568 | tf_op jit(solution)/shard_map/while/body/eval_jaxpr/ppermute | solution.py:9
  17.0 0.2 convolution_select_fusion.3
  17.1 0.7 scatter_fusion
  17.9 0.1 collective-permute-start
  18.0 0.6 dynamic_slice.64
  18.6 0.6 iota_compare_fusion.3
  19.2 2.4 %collective-permute-done = bf16[128,256]{1,0:T(8,128)(2,1)S(1)} collective-permute-done((bf16[128,256]{1,0:T(8,128)(2,1)S(1)}, bf16[128,256]{1,0:T(8,128)(2,1)S(1)}, u32[]{:S(2)}, u32[]{:S(2)}) %collective-permute-start) | collective-permute-done | bytes 65568 | tf_op jit(solution)/shard_map/while/body/eval_jaxpr/ppermute | solution.py:9
  21.6 0.2 convolution_select_fusion.3
  21.8 0.7 scatter_fusion
  22.5 0.1 collective-permute-start
  22.6 0.6 dynamic_slice.64
  23.2 0.6 iota_compare_fusion.3
  23.9 2.4 %collective-permute-done = bf16[128,256]{1,0:T(8,128)(2,1)S(1)} collective-permute-done((bf16[128,256]{1,0:T(8,128)(2,1)S(1)}, bf16[128,256]{1,0:T(8,128)(2,1)S(1)}, u32[]{:S(2)}, u32[]{:S(2)}) %collective-permute-start) | collective-permute-done | bytes 65568 | tf_op jit(solution)/shard_map/while/body/eval_jaxpr/ppermute | solution.py:9
  26.3 0.2 convolution_select_fusion.3
  26.4 0.7 scatter_fusion
  27.2 0.0 copy-start.1
  27.2 0.0 copy-start.4
  27.2 1.0 copy-done.1
  28.1 0.0 reduce-scatter.2.cloned.1.call-update
  28.2 0.0 all-reduce.2.cloned.1.call-start
  28.2 65.5 %reduce-scatter.2.cloned.1.call-done = f32[128,256]{1,0:T(8,128)} async-done(((f32[1024,256]{1,0:T(8,128)}), f32[128,256]{1,0:T(8,128)}) %reduce-scatter.2.cloned.1.call-update) | async-done | bytes 131088 | tf_op jit(solution)/shard_map/reduce_scatter | solution.py:46
  93.8 0.0 copy-done.4
  93.8 1.8 convolution_bitcast_fusion
  95.6 0.0 copy-start.2
  95.6 0.0 all-reduce.2.cloned.1.call-update
  95.6 0.0 copy-done
  95.6 0.9 copy-done.2
  96.5 0.8 convolution_convert_fusion
  97.3 127.5 %all-reduce.2.cloned.1.call-done = f32[256,256]{0,1:T(8,128)} async-done(((f32[256,256]{0,1:T(8,128)}), f32[256,256]{0,1:T(8,128)}) %all-reduce.2.cloned.1.call-update) | async-done | bytes 262160 | tf_op jit(solution)/shard_map/psum | solution.py:60
  224.8 1.0 broadcast_multiply_fusion
  225.8 0.8 copy.12
  (8 shorter events, 0.1 us)
Async XLA Ops:
  7.2 88.4 %copy-start = (bf16[256,256]{1,0:T(8,128)(2,1)S(1)}, bf16[256,256]{1,0:T(8,128)(2,1)}, u32[]{:S(2)}) copy-start(bf16[256,256]{1,0:T(8,128)(2,1)} %param.12) | copy-start | bytes 393220
  7.2 86.6 %reduce-scatter.2.cloned.1.call-start = ((), (), s32[]{:S(2)}) async-start(), calls=%async_computation.1 | async-start | bytes 1179648 | tf_op jit(solution)/shard_map/reduce_scatter | solution.py:46
  7.2 0.7 copy-start.7
  8.5 0.7 copy-start.6
  9.5 1.2 copy-start.3
  9.5 1.2 copy-start.5
  12.6 4.4 %collective-permute-start = (bf16[128,256]{1,0:T(8,128)(2,1)S(1)}, bf16[128,256]{1,0:T(8,128)(2,1)S(1)}, u32[]{:S(2)}, u32[]{:S(2)}) collective-permute-start(bf16[128,256]{1,0:T(8,128)(2,1)S(1)} %get-tuple-element.297), channel_id=1, source_target_pairs={{0,8},{8,16},{16,24},{24,0},{1,9},{9,17},{17,25},{25,1},{2,10},{10... | collective-permute-start | bytes 196616 | tf_op jit(solution)/shard_map/while/body/eval_jaxpr/ppermute | solution.py:9
  17.9 3.7 %collective-permute-start = (bf16[128,256]{1,0:T(8,128)(2,1)S(1)}, bf16[128,256]{1,0:T(8,128)(2,1)S(1)}, u32[]{:S(2)}, u32[]{:S(2)}) collective-permute-start(bf16[128,256]{1,0:T(8,128)(2,1)S(1)} %get-tuple-element.297), channel_id=1, source_target_pairs={{0,8},{8,16},{16,24},{24,0},{1,9},{9,17},{17,25},{25,1},{2,10},{10... | collective-permute-start | bytes 196616 | tf_op jit(solution)/shard_map/while/body/eval_jaxpr/ppermute | solution.py:9
  22.5 3.7 %collective-permute-start = (bf16[128,256]{1,0:T(8,128)(2,1)S(1)}, bf16[128,256]{1,0:T(8,128)(2,1)S(1)}, u32[]{:S(2)}, u32[]{:S(2)}) collective-permute-start(bf16[128,256]{1,0:T(8,128)(2,1)S(1)} %get-tuple-element.297), channel_id=1, source_target_pairs={{0,8},{8,16},{16,24},{24,0},{1,9},{9,17},{17,25},{25,1},{2,10},{10... | collective-permute-start | bytes 196616 | tf_op jit(solution)/shard_map/while/body/eval_jaxpr/ppermute | solution.py:9
  27.2 1.0 copy-start.1
  27.2 66.6 %copy-start.4 = (bf16[128,256]{1,0:T(8,128)(2,1)S(1)}, bf16[128,256]{1,0:T(8,128)(2,1)}, u32[]{:S(2)}) copy-start(bf16[128,256]{1,0:T(8,128)(2,1)} %param.11) | copy-start | bytes 196612
  28.2 196.6 %all-reduce.2.cloned.1.call-start = ((), (), s32[]{:S(2)}) async-start(), calls=%async_computation.2 | async-start | bytes 524288 | tf_op jit(solution)/shard_map/psum | solution.py:60
  95.6 0.9 copy-start.2
Sparse Core Ops, SparseCore 0:
  28.3 65.4 reduce-scatter.1
  100.7 124.0 all-reduce.1
where the time goes:
time: 234 us; the launch traced here: 233 us
  waiting for transfers between devices  200 us (85%)
  between operations  14.2 us (6%)
  local copies, waits for them, and re-layouts  7.35 us (3%)
  other arithmetic  6.37 us (3%)
  matrix products  4.19 us (2%)
    psum x1, waiting for transfers between devices, body(): grad_weight = lax.psum(weight_term, ('blk', 'rep')) * total_nodes ** (-0.5)  127 us
    reduce_scatter x1, waiting for transfers between devices, body(): lax.psum_scatter(partial_value.reshape(block_tiles * tile_height, width),...  65.5 us
    ppermute x3, waiting for transfers between devices, from_behind(): lax.ppermute(array, axis, [(i, (i + by) % devices) for i in range(devices)])  7.38 us
  transfers between devices with their start and end apart: 5, of which 5 were waited for; matrix products, arithmetic and copies ran while one was open for 2% of the time, Pallas kernels for 0%

commit v1 on v0

v1 whole, which is shorter than its diff:
```python
import functools

import jax
import jax.numpy as jnp
from jax import lax
from jax.experimental import pallas as pl
from jax.experimental.pallas import tpu as pltpu
from jax.sharding import PartitionSpec as P

MESH = pl.DeviceIdType.MESH
UNROLL = 8
GROUP = 4


def loop(low, high, step):
    if high - low <= UNROLL:
        for index in range(low, high):
            step(index)
    else:
        lax.fori_loop(low, high, lambda index, carry: (step(index), carry)[1], 0)


def fold(count, step, start):
    if count <= UNROLL:
        for index in range(count):
            start = step(index, start)
        return start
    return lax.fori_loop(0, count, step, start)


def remote(source, target, send, receive, device):
    return pltpu.make_async_remote_copy(
        src_ref=source,
        dst_ref=target,
        send_sem=send,
        recv_sem=receive,
        device_id=device,
        device_id_type=MESH,
    )


def kernel(
    nblk, nrep, scale,
    rows_ref, counts_ref, grad_ref, relu_ref, feat_ref, weight_ref, tiles_ref,
    gf_ref, gw_ref,
    pieces, turned, feat_t, away, arrived, own, terms, terms_low, share_in, block_sum, final,
    gs, gr, rs, rr, ts, tr, bs, br, fs, fr,
):
    me_b = lax.axis_index("blk")
    me_r = lax.axis_index("rep")
    slot_count = tiles_ref.shape[2]
    rows = terms.shape[1]
    halves = gw_ref.shape[1] // 128
    per_half = nrep // halves

    barrier = pltpu.get_barrier_semaphore()

    def greet_b(d):
        pl.semaphore_signal(barrier, inc=1, device_id={"blk": lax.rem(me_b + d, nblk)}, device_id_type=MESH)

    def greet_r(e):
        pl.semaphore_signal(barrier, inc=1, device_id={"rep": lax.rem(me_r + e, nrep)}, device_id_type=MESH)

    loop(1, nblk, greet_b)
    loop(1, nrep, greet_r)
    grad = grad_ref[...]
    pieces[0] = jnp.where(relu_ref[...] == 1, grad, jnp.zeros_like(grad))
    pl.semaphore_wait(barrier, nblk + nrep - 2)

    def gather(d):
        return remote(pieces.at[0], pieces.at[d], gs.at[d], gr.at[d], {"blk": lax.rem(me_b + d, nblk)})

    loop(1, nblk, lambda d: gather(d).start())

    def turn(d):
        source = lax.rem(me_b - d + nblk, nblk)
        for k in range(slot_count):
            turned[d, k] = tiles_ref[0, source, k].T

    loop(0, nblk, turn)
    feat_t[...] = feat_ref[...].T
    loop(1, nblk, lambda d: gather(d).wait_recv())

    def partial(t):
        def part(g, total):
            right = pieces[pl.ds(g * GROUP, GROUP)].reshape(GROUP * pieces.shape[1], pieces.shape[2])
            for k in range(slot_count):
                left = []
                for i in range(GROUP):
                    d = g * GROUP + i
                    source = lax.rem(me_b - d + nblk, nblk)
                    live = (rows_ref[0, source, k] == t) & (k < counts_ref[0, source])
                    here = turned[d, k]
                    gate = jnp.full((1, here.shape[1]), live.astype(jnp.float32)).astype(here.dtype)
                    left.append(here * gate)
                total = total + jnp.dot(jnp.concatenate(left, axis=1), right, preferred_element_type=jnp.float32)
            return total

        return fold(nblk // GROUP, part, jnp.zeros(own.shape, jnp.float32))

    def scatter(e):
        return remote(away.at[e], arrived.at[e], rs.at[e], rr.at[e], {"rep": lax.rem(me_r + e, nrep)})

    def send_part(e):
        away[e] = partial(lax.rem(me_r + e, nrep)).astype(away.dtype)
        scatter(e).start()

    loop(1, nrep, send_part)
    own[...] = partial(me_r)

    def take(e):
        scatter(e).wait_recv()
        own[...] += arrived[e].astype(jnp.float32)

    loop(1, nrep, take)
    aggregated = own[...].astype(jnp.bfloat16)

    term = jnp.dot(feat_t[...], aggregated, preferred_element_type=jnp.float32) * scale
    for p in range(nrep):
        half, at = p // per_half, (p % per_half) * rows
        cut = term[at:at + rows, half * 128:half * 128 + 128]
        terms[p] = cut
        terms_low[p] = cut.astype(terms_low.dtype)

    def share(e):
        other = lax.rem(me_r + e, nrep)
        return remote(terms_low.at[other], share_in.at[e], ts.at[e], tr.at[e], {"rep": other})

    loop(1, nrep, lambda e: share(e).start())
    gf_ref[...] = lax.dot_general(
        aggregated, weight_ref[...], (((1,), (1,)), ((), ())), preferred_element_type=jnp.float32
    ).astype(gf_ref.dtype)

    def take_share(index, total):
        e = index + 1
        share(e).wait_recv()
        return total + share_in[e].astype(jnp.float32)

    block_sum[me_b] = fold(nrep - 1, take_share, terms[me_r]).astype(block_sum.dtype)

    def across(d):
        return remote(block_sum.at[me_b], block_sum.at[me_b], bs.at[d], br.at[d], {"blk": lax.rem(me_b + d, nblk)})

    loop(1, nblk, lambda d: across(d).start())
    loop(1, nblk, lambda d: across(d).wait_recv())
    whole = fold(nblk, lambda b, total: total + block_sum[b].astype(jnp.float32), jnp.zeros(terms.shape[1:], jnp.float32))
    final[me_r] = whole.astype(final.dtype)

    def spread(e):
        return remote(final.at[me_r], final.at[me_r], fs.at[e], fr.at[e], {"rep": lax.rem(me_r + e, nrep)})

    loop(1, nrep, lambda e: spread(e).start())
    loop(1, nrep, lambda e: spread(e).wait_recv())
    for p in range(nrep):
        half, at = p // per_half, (p % per_half) * rows
        gw_ref[at:at + rows, half * 128:half * 128 + 128] = final[p].astype(jnp.float32)

    loop(1, nblk, lambda d: gather(d).wait_send())
    loop(1, nrep, lambda e: scatter(e).wait_send())
    loop(1, nrep, lambda e: share(e).wait_send())
    loop(1, nblk, lambda d: across(d).wait_send())
    loop(1, nrep, lambda e: spread(e).wait_send())


def body(grad_out, relu_bits, features, weight, tiles, tile_rows, tile_counts):
    nblk = lax.axis_size("blk")
    nrep = lax.axis_size("rep")
    rows, width = grad_out.shape
    depth = features.shape[1]
    slots = tiles.shape[2]
    rows_share = depth * width // (nrep * 128)
    low, high = jnp.bfloat16, jnp.float32
    vmem = pl.BlockSpec(memory_space=pltpu.VMEM)
    smem = pl.BlockSpec(memory_space=pltpu.SMEM)
    dma = pltpu.SemaphoreType.DMA
    return pl.pallas_call(
        functools.partial(kernel, nblk, nrep, float(rows * nrep * nblk) ** -0.5),
        out_shape=(
            jax.ShapeDtypeStruct((rows, depth), low),
            jax.ShapeDtypeStruct((depth, width), high),
        ),
        in_specs=[smem, smem, vmem, vmem, vmem, vmem, vmem],
        out_specs=(vmem, vmem),
        scratch_shapes=[
            pltpu.VMEM((nblk, rows, width), low),
            pltpu.VMEM((nblk, slots, tiles.shape[4], tiles.shape[3]), low),
            pltpu.VMEM((depth, rows), low),
            pltpu.VMEM((nrep, rows, width), low),
            pltpu.VMEM((nrep, rows, width), low),
            pltpu.VMEM((rows, width), high),
            pltpu.VMEM((nrep, rows_share, 128), high),
            pltpu.VMEM((nrep, rows_share, 128), low),
            pltpu.VMEM((nrep, rows_share, 128), low),
            pltpu.VMEM((nblk, rows_share, 128), low),
            pltpu.VMEM((nrep, rows_share, 128), low),
            dma((nblk,)), dma((nblk,)),
            dma((nrep,)), dma((nrep,)),
            dma((nrep,)), dma((nrep,)),
            dma((nblk,)), dma((nblk,)),
            dma((nrep,)), dma((nrep,)),
        ],
        compiler_params=pltpu.CompilerParams(
            collective_id=0, has_side_effects=True, vmem_limit_bytes=40 * 1024 * 1024
        ),
        cost_estimate=pl.CostEstimate(flops=10**9, bytes_accessed=10**6, transcendentals=0),
    )(tile_rows, tile_counts, grad_out, relu_bits, features, weight, tiles)


def solution(mesh):
    return jax.shard_map(
        body,
        mesh=mesh,
        in_specs=(
            P(("blk", "rep"), None),
            P(("blk", "rep"), None),
            P(("blk", "rep"), None),
            P(),
            P(("blk", "rep"), None, None, None, None),
            P(("blk", "rep"), None, None),
            P(("blk", "rep"), None),
        ),
        out_specs=(P(("blk", "rep"), None), P()),
        check_vma=False,
    )
```

time: 234 us -> 45 us (0.19)
  waiting for transfers between devices: 200 us -> 0 us
  Pallas kernels: 0 us -> 37.5 us
  between operations: 14.2 us -> 0.65 us
  other arithmetic: 6.37 us -> 0 us
  matrix products: 4.19 us -> 0 us
    psum x1 -> x0, waiting for transfers between devices: 127 us -> none  [body(): grad_weight = lax.psum(weight_term, ('blk', 'rep')) * total_nodes ** (-0.5)]
    reduce_scatter x1 -> x0, waiting for transfers between devices: 65.5 us -> none  [body(): lax.psum_scatter(partial_value.reshape(block_tiles * tile_height, width),...]
    pallas_call x0 -> x1, Pallas kernels: none -> 37.5 us  [body(): pl.pallas_call(functools.partial(kernel, nblk, nrep, float(rows * nrep *...]
    ppermute x3 -> x0, waiting for transfers between devices: 7.38 us -> none  [from_behind(): lax.ppermute(array, axis, [(i, (i + by) % devices) for i in range(devices)])]
    dot_general x6 -> x0, matrix products: 4.19 us -> none  [the longest x1 1.82 us: body(): lax.dot_general(features, aggregated, (((0,), (0,)), ((), ())), preferred...]
    scatter-add x4 -> x0, other arithmetic: 2.78 us -> none  [accumulate(): return partial_value.at[rows_set].add(prods)]
    dynamic_slice x5 -> x0, local copies, waits for them, and re-layouts: 2.62 us -> none  [the longest x4 2.43 us: accumulate(): count = lax.dynamic_index_in_dim(my_counts, source, 0, keepdims=False)]
    lt x4 -> x0, other arithmetic: 2.56 us -> none  [accumulate(): live = (slots < count)[:, None, None]]
  transfers between devices with their start and end apart: 5 -> 0, of which waited for: 5 -> 0; matrix products, arithmetic and copies ran while one was open for 2% -> 0% of each run, Pallas kernels for 0% -> 0%
where the time goes in v1:
time: 45 us; the launch traced here: 44.7 us
  Pallas kernels  37.5 us (83%)
  local copies, waits for them, and re-layouts  6.54 us (15%)
  between operations  0.65 us (1%)
    pallas_call x1, Pallas kernels, body(): pl.pallas_call(functools.partial(kernel, nblk, nrep, float(rows * nrep *...  37.5 us
    unnamed x15, local copies, waits for them, and re-layouts  6.54 us

profile of v1, /device:TPU:0, one launch (start us, length us, event | category | flops | bytes accessed | tf_op | source)
XLA Modules:
  0.0 44.7 jit_solution(10554509317560156219)
XLA Ops:
  0.6 0.0 copy-start.5
  0.6 0.8 %copy.9.rows_ref = s32[1,4,2]{2,1,0:T(4,128)S(1)} copy(s32[1,4,2]{1,2,0:T(2,128)} %param.12) | data formatting | bytes 64 | tf_op args[5]
  1.4 0.0 copy-done.5
  1.4 0.0 copy-start
  1.4 0.9 %copy-done = bf16[1,4,2,128,128]{4,3,2,1,0:T(8,128)(2,1)S(1)} copy-done((bf16[1,4,2,128,128]{4,3,2,1,0:T(8,128)(2,1)S(1)}, bf16[1,4,2,128,128]{4,3,2,1,0:T(8,128)(2,1)}, u32[]{:S(2)}) %copy-start) | copy-done | bytes 262168
  2.4 0.0 copy-start.1
  2.4 0.9 %copy-done.1 = s32[128,256]{1,0:T(8,128)S(1)} copy-done((s32[128,256]{1,0:T(8,128)S(1)}, s32[128,256]{1,0:T(8,128)}, u32[]{:S(2)}) %copy-start.1) | copy-done | bytes 131096
  3.3 0.0 copy-start.2
  3.3 0.9 %copy-done.2 = bf16[256,256]{1,0:T(8,128)(2,1)S(1)} copy-done((bf16[256,256]{1,0:T(8,128)(2,1)S(1)}, bf16[256,256]{1,0:T(8,128)(2,1)}, u32[]{:S(2)}) %copy-start.2) | copy-done | bytes 131096
  4.2 0.0 copy-start.3
  4.2 0.8 %copy-done.3 = bf16[128,256]{1,0:T(8,128)(2,1)S(1)} copy-done((bf16[128,256]{1,0:T(8,128)(2,1)S(1)}, bf16[128,256]{1,0:T(8,128)(2,1)}, u32[]{:S(2)}) %copy-start.3) | copy-done | bytes 65560
  5.0 0.0 copy-start.4
  5.0 0.8 %copy-done.4 = bf16[128,256]{1,0:T(8,128)(2,1)S(1)} copy-done((bf16[128,256]{1,0:T(8,128)(2,1)S(1)}, bf16[128,256]{1,0:T(8,128)(2,1)}, u32[]{:S(2)}) %copy-start.4) | copy-done | bytes 65560
  5.9 37.5 %shard_map.86 = (bf16[128,256]{1,0:T(8,128)(2,1)S(1)}, f32[256,256]{1,0:T(8,128)S(1)}) custom-call(s32[1,4,2]{2,1,0:T(4,128)S(1)} %copy.9.rows_ref, s32[1,4]{1,0:T(1,128)S(1)} %copy-done.5, bf16[128,256]{1,0:T(8,128)(2,1)S(1)} %copy-done.3, s32[128,256]{1,0:T(8,128)S(1)} %copy-done.1, bf16[128,256]{1,0:T(8,128)(2,1)S(1)} %copy-done.4, ...), custom_call_target="tpu_custom_call" | custom-call | flops 1000000000 | bytes 1000000 | tf_op jit(solution)/shard_map/pallas_call | solution.py:176
  43.4 0.6 %copy.12 = bf16[128,256]{1,0:T(8,128)(2,1)} copy(bf16[128,256]{1,0:T(8,128)(2,1)S(1)} %get-tuple-element.4) | data formatting | bytes 131072
  44.0 0.7 %copy.13 = f32[256,256]{1,0:T(8,128)} copy(f32[256,256]{1,0:T(8,128)S(1)} %get-tuple-element.5) | data formatting | bytes 524288
Async XLA Ops:
  0.6 0.8 %copy-start.5 = (s32[1,4]{1,0:T(1,128)S(1)}, s32[1,4]{1,0:T(1,128)}, u32[]{:S(2)}) copy-start(s32[1,4]{1,0:T(1,128)} %counts_ref.1) | copy-start | bytes 52
  1.4 1.0 %copy-start = (bf16[1,4,2,128,128]{4,3,2,1,0:T(8,128)(2,1)S(1)}, bf16[1,4,2,128,128]{4,3,2,1,0:T(8,128)(2,1)}, u32[]{:S(2)}) copy-start(bf16[1,4,2,128,128]{4,3,2,1,0:T(8,128)(2,1)} %tiles_ref.1) | copy-start | bytes 786436
  2.4 0.9 %copy-start.1 = (s32[128,256]{1,0:T(8,128)S(1)}, s32[128,256]{1,0:T(8,128)}, u32[]{:S(2)}) copy-start(s32[128,256]{1,0:T(8,128)} %relu_ref.1) | copy-start | bytes 393220
  3.3 0.9 %copy-start.2 = (bf16[256,256]{1,0:T(8,128)(2,1)S(1)}, bf16[256,256]{1,0:T(8,128)(2,1)}, u32[]{:S(2)}) copy-start(bf16[256,256]{1,0:T(8,128)(2,1)} %weight_ref.1) | copy-start | bytes 393220
  4.2 0.8 %copy-start.3 = (bf16[128,256]{1,0:T(8,128)(2,1)S(1)}, bf16[128,256]{1,0:T(8,128)(2,1)}, u32[]{:S(2)}) copy-start(bf16[128,256]{1,0:T(8,128)(2,1)} %grad_ref.1) | copy-start | bytes 196612
  5.0 0.8 %copy-start.4 = (bf16[128,256]{1,0:T(8,128)(2,1)S(1)}, bf16[128,256]{1,0:T(8,128)(2,1)}, u32[]{:S(2)}) copy-start(bf16[128,256]{1,0:T(8,128)(2,1)} %feat_ref.1) | copy-start | bytes 196612

commit v2 on v1

v2 whole, which is shorter than its diff:
```python
import functools

import jax
import jax.numpy as jnp
from jax import lax
from jax.experimental import pallas as pl
from jax.experimental.pallas import tpu as pltpu
from jax.sharding import PartitionSpec as P

MESH = pl.DeviceIdType.MESH
UNROLL = 8
GROUP = 4


def loop(low, high, step):
    if high - low <= UNROLL:
        for index in range(low, high):
            step(index)
    else:
        lax.fori_loop(low, high, lambda index, carry: (step(index), carry)[1], 0)


def fold(count, step, start):
    if count <= UNROLL:
        for index in range(count):
            start = step(index, start)
        return start
    return lax.fori_loop(0, count, step, start)


def remote(source, target, send, receive, device):
    return pltpu.make_async_remote_copy(
        src_ref=source,
        dst_ref=target,
        send_sem=send,
        recv_sem=receive,
        device_id=device,
        device_id_type=MESH,
    )


def kernel(
    nblk, nrep, scale,
    rows_hbm, counts_hbm, grad_hbm, relu_hbm, feat_hbm, weight_hbm, tiles_hbm,
    gf_ref, gw_ref,
    rows_ref, counts_ref, grad_ref, relu_ref, feat_ref, weight_ref, tiles_ref, inputs,
    pieces, turned, feat_t, away, arrived, kept, mixed, gathered, own,
    terms, terms_low, share_in, block_sum, block_low, part_in, final,
    gs, gr, ps, pr, rs, rr, ts, tr, bs, br, ks, kr, fs, fr,
):
    me_b = lax.axis_index("blk")
    me_r = lax.axis_index("rep")
    slot_count = tiles_ref.shape[2]
    rows = terms.shape[1]
    halves = gw_ref.shape[1] // 128
    per_half = nblk // halves
    outer = nrep // 2
    me_o, me_i = me_r // 2, lax.rem(me_r, 2)

    barrier = pltpu.get_barrier_semaphore()

    def greet_b(d):
        pl.semaphore_signal(barrier, inc=1, device_id={"blk": lax.rem(me_b + d, nblk)}, device_id_type=MESH)

    def greet_r(e):
        pl.semaphore_signal(barrier, inc=1, device_id={"rep": lax.rem(me_r + e, nrep)}, device_id_type=MESH)

    loop(1, nrep, greet_r)
    loop(1, nblk, greet_b)
    order = (
        (grad_hbm, grad_ref), (relu_hbm, relu_ref), (tiles_hbm, tiles_ref), (rows_hbm, rows_ref),
        (counts_hbm, counts_ref), (feat_hbm, feat_ref), (weight_hbm, weight_ref),
    )
    load = [pltpu.make_async_copy(there, here, inputs.at[i]) for i, (there, here) in enumerate(order)]
    for copy in load:
        copy.start()
    load[0].wait()
    load[1].wait()
    grad = grad_ref[...]
    pieces[0] = jnp.where(relu_ref[...] == 1, grad, jnp.zeros_like(grad))
    pl.semaphore_wait(barrier, nblk + nrep - 2)

    def gather(d):
        return remote(pieces.at[0], pieces.at[d], gs.at[d], gr.at[d], {"blk": lax.rem(me_b + d, nblk)})

    loop(1, nblk, lambda d: gather(d).start())

    load[2].wait()

    def turn(d):
        source = lax.rem(me_b - d + nblk, nblk)
        for k in range(slot_count):
            turned[d, k] = tiles_ref[0, source, k].T

    loop(0, nblk, turn)
    for copy in load[3:]:
        copy.wait()
    feat_t[...] = feat_ref[...].T
    loop(1, nblk, lambda d: gather(d).wait_recv())

    def partial(t):
        def part(g, total):
            right = pieces[pl.ds(g * GROUP, GROUP)].reshape(GROUP * pieces.shape[1], pieces.shape[2])
            for k in range(slot_count):
                left = []
                for i in range(GROUP):
                    d = g * GROUP + i
                    source = lax.rem(me_b - d + nblk, nblk)
                    live = (rows_ref[0, k, source] == t) & (k < counts_ref[0, source])
                    here = turned[d, k]
                    gate = jnp.full((1, here.shape[1]), live.astype(jnp.float32)).astype(here.dtype)
                    left.append(here * gate)
                total = total + jnp.dot(jnp.concatenate(left, axis=1), right, preferred_element_type=jnp.float32)
            return total

        return fold(nblk // GROUP, part, jnp.zeros(own.shape, jnp.float32))

    def flip(q):
        total, bit = 0, 1
        while bit < outer:
            total = total + lax.rem(me_o // bit + q // bit, 2) * bit
            bit *= 2
        return total

    def pair(q):
        return remote(away.at[q], arrived.at[q], ps.at[q], pr.at[q], {"rep": me_o * 2 + 1 - me_i})

    def scatter(q):
        return remote(mixed.at[q], gathered.at[q], rs.at[q], rr.at[q], {"rep": flip(q) * 2 + me_i})

    def send_pair(step):
        q = outer - 1 - step
        away[q] = partial(flip(q) * 2 + 1 - me_i).astype(away.dtype)
        pair(q).start()
        kept[q] = partial(flip(q) * 2 + me_i)

    loop(0, outer, send_pair)

    def send_part(step):
        q = outer - 1 - step
        pair(q).wait_recv()
        mixed[q] = (kept[q] + arrived[q].astype(jnp.float32)).astype(mixed.dtype)
        scatter(q).start()

    loop(0, outer - 1, send_part)
    pair(0).wait_recv()
    own[...] = kept[0] + arrived[0].astype(jnp.float32)

    def take(step):
        q = step + 1
        scatter(q).wait_recv()
        own[...] += gathered[q].astype(jnp.float32)

    loop(0, outer - 1, take)
    aggregated = own[...].astype(jnp.bfloat16)

    term = jnp.dot(feat_t[...], aggregated, preferred_element_type=jnp.float32) * scale
    for p in range(nblk):
        half, at = p // per_half, (p % per_half) * rows
        cut = term[at:at + rows, half * 128:half * 128 + 128]
        terms[p] = cut
        terms_low[p] = cut.astype(terms_low.dtype)

    def share(d):
        other = lax.rem(me_b + d, nblk)
        return remote(terms_low.at[other], share_in.at[d], ts.at[d], tr.at[d], {"blk": other})

    loop(1, nblk, lambda d: share(d).start())
    gf_ref[...] = lax.dot_general(
        aggregated, weight_ref[...], (((1,), (1,)), ((), ())), preferred_element_type=jnp.float32
    ).astype(gf_ref.dtype)

    def take_share(index, total):
        share(index + 1).wait_recv()
        return total + share_in[index + 1].astype(jnp.float32)

    block_sum[...] = fold(nblk - 1, take_share, terms[me_b])
    part_rows = part_in.shape[1]
    split = part_rows < rows
    if split:
        block_low[...] = block_sum[...].astype(block_low.dtype)
        mine = pl.ds(pl.multiple_of(me_r * part_rows, part_rows), part_rows)

        def across(e):
            other = lax.rem(me_r + e, nrep)
            theirs = pl.ds(pl.multiple_of(other * part_rows, part_rows), part_rows)
            return remote(block_low.at[theirs], part_in.at[e], bs.at[e], br.at[e], {"rep": other})

        def take_part(index, total):
            across(index + 1).wait_recv()
            return total + part_in[index + 1].astype(jnp.float32)

        loop(1, nrep, lambda e: across(e).start())
        final[me_b, mine] = fold(nrep - 1, take_part, block_sum[mine]).astype(final.dtype)

        def regain(e):
            place = final.at[me_b, mine]
            return remote(place, place, ks.at[e], kr.at[e], {"rep": lax.rem(me_r + e, nrep)})

        loop(1, nrep, lambda e: regain(e).start())
        loop(1, nrep, lambda e: regain(e).wait_recv())
    else:
        part_in[me_r] = block_sum[...].astype(part_in.dtype)

        def across(e):
            place = part_in.at[me_r]
            return remote(place, place, bs.at[e], br.at[e], {"rep": lax.rem(me_r + e, nrep)})

        loop(1, nrep, lambda e: across(e).start())
        loop(1, nrep, lambda e: across(e).wait_recv())
        final[me_b] = fold(
            nrep, lambda r, total: total + part_in[r].astype(jnp.float32), jnp.zeros(block_sum.shape, jnp.float32)
        ).astype(final.dtype)

    def spread(d):
        return remote(final.at[me_b], final.at[me_b], fs.at[d], fr.at[d], {"blk": lax.rem(me_b + d, nblk)})

    loop(1, nblk, lambda d: spread(d).start())
    loop(1, nblk, lambda d: spread(d).wait_recv())
    for p in range(nblk):
        half, at = p // per_half, (p % per_half) * rows
        gw_ref[at:at + rows, half * 128:half * 128 + 128] = final[p].astype(jnp.float32)

    loop(1, nblk, lambda d: gather(d).wait_send())
    loop(0, outer, lambda q: pair(q).wait_send())
    loop(1, outer, lambda q: scatter(q).wait_send())
    loop(1, nblk, lambda d: share(d).wait_send())
    loop(1, nrep, lambda e: across(e).wait_send())
    if split:
        loop(1, nrep, lambda e: regain(e).wait_send())
    loop(1, nblk, lambda d: spread(d).wait_send())


def body(grad_out, relu_bits, features, weight, tiles, tile_rows, tile_counts):
    nblk = lax.axis_size("blk")
    nrep = lax.axis_size("rep")
    rows, width = grad_out.shape
    depth = features.shape[1]
    slots = tiles.shape[2]
    rows_share = depth * width // (nblk * 128)
    outer = nrep // 2
    rows_part = rows_share // nrep if rows_share % (16 * nrep) == 0 else rows_share
    low, high = jnp.bfloat16, jnp.float32
    vmem = pl.BlockSpec(memory_space=pltpu.VMEM)
    hbm = pl.BlockSpec(memory_space=pltpu.HBM)
    dma = pltpu.SemaphoreType.DMA
    return pl.pallas_call(
        functools.partial(kernel, nblk, nrep, float(rows * nrep * nblk) ** -0.5),
        out_shape=(
            jax.ShapeDtypeStruct((rows, depth), low),
            jax.ShapeDtypeStruct((depth, width), high),
        ),
        in_specs=[hbm] * 7,
        out_specs=(vmem, vmem),
        scratch_shapes=[
            pltpu.SMEM((1, slots, nblk), jnp.int32),
            pltpu.SMEM((1, nblk), jnp.int32),
            pltpu.VMEM((rows, width), low),
            pltpu.VMEM((rows, width), jnp.int32),
            pltpu.VMEM((rows, depth), low),
            pltpu.VMEM((depth, width), low),
            pltpu.VMEM(tiles.shape, low),
            dma((7,)),
            pltpu.VMEM((nblk, rows, width), low),
            pltpu.VMEM((nblk, slots, tiles.shape[4], tiles.shape[3]), low),
            pltpu.VMEM((depth, rows), low),
            pltpu.VMEM((outer, rows, width), low),
            pltpu.VMEM((outer, rows, width), low),
            pltpu.VMEM((outer, rows, width), high),
            pltpu.VMEM((outer, rows, width), low),
            pltpu.VMEM((outer, rows, width), low),
            pltpu.VMEM((rows, width), high),
            pltpu.VMEM((nblk, rows_share, 128), high),
            pltpu.VMEM((nblk, rows_share, 128), low),
            pltpu.VMEM((nblk, rows_share, 128), low),
            pltpu.VMEM((rows_share, 128), high),
            pltpu.VMEM((rows_share, 128), low),
            pltpu.VMEM((nrep, rows_part, 128), low),
            pltpu.VMEM((nblk, rows_share, 128), low),
            dma((nblk,)), dma((nblk,)),
            dma((outer,)), dma((outer,)),
            dma((outer,)), dma((outer,)),
            dma((nblk,)), dma((nblk,)),
            dma((nrep,)), dma((nrep,)),
            dma((nrep,)), dma((nrep,)),
            dma((nblk,)), dma((nblk,)),
        ],
        compiler_params=pltpu.CompilerParams(
            collective_id=0, has_side_effects=True, vmem_limit_bytes=64 * 1024 * 1024 - 65536
        ),
        cost_estimate=pl.CostEstimate(flops=10**9, bytes_accessed=10**6, transcendentals=0),
    )(jnp.swapaxes(tile_rows, 1, 2), tile_counts, grad_out, relu_bits, features, weight, tiles)


def solution(mesh):
    return jax.shard_map(
        body,
        mesh=mesh,
        in_specs=(
            P(("blk", "rep"), None),
            P(("blk", "rep"), None),
            P(("blk", "rep"), None),
            P(),
            P(("blk", "rep"), None, None, None, None),
            P(("blk", "rep"), None, None),
            P(("blk", "rep"), None),
        ),
        out_specs=(P(("blk", "rep"), None), P()),
        check_vma=False,
    )
```

time: 45 us -> 40.5 us (0.900)
  local copies, waits for them, and re-layouts: 6.54 us -> 3.14 us
  Pallas kernels: 37.5 us -> 36.5 us
    unnamed x15 -> x2, local copies, waits for them, and re-layouts: 6.54 us -> 3.14 us
    pallas_call x1, Pallas kernels: 37.5 us -> 36.5 us  [body(): pl.pallas_call(functools.partial(kernel, nblk, nrep, float(rows * nrep *...]
where the time goes in v2:
time: 40.5 us; the launch traced here: 40.3 us
  Pallas kernels  36.5 us (90%)
  local copies, waits for them, and re-layouts  3.14 us (8%)
  between operations  0.64 us (2%)
    pallas_call x1, Pallas kernels, body(): pl.pallas_call(functools.partial(kernel, nblk, nrep, float(rows * nrep *...  36.5 us
    unnamed x2, local copies, waits for them, and re-layouts  3.14 us

profile of v2, /device:TPU:0, one launch (start us, length us, event | category | flops | bytes accessed | tf_op | source)
XLA Modules:
  0.0 40.3 jit_solution(1778582001629254309)
XLA Ops:
  0.6 36.5 %shard_map.86 = (bf16[128,256]{1,0:T(8,128)(2,1)}, f32[256,256]{1,0:T(8,128)}) custom-call(s32[1,2,4]{2,1,0:T(2,128)} %bitcast.1, s32[1,4]{1,0:T(1,128)} %counts_hbm.1, bf16[128,256]{1,0:T(8,128)(2,1)} %grad_hbm.1, s32[128,256]{1,0:T(8,128)} %relu_hbm.1, bf16[128,256]{1,0:T(8,128)(2,1)} %feat_hbm.1, bf16[256,256]{1,0:T(8,128)(2,1)} %weight_hbm.1, ...), custom_call_target="tpu_custom_call" | custom-call | flops 1000000000 | bytes 1000000 | tf_op jit(solution)/shard_map/pallas_call | solution.py:247
  37.2 1.5 %copy.11 = bf16[128,256]{1,0:T(8,128)(2,1)} copy(bf16[128,256]{1,0:T(8,128)(2,1)} %get-tuple-element.4) | data formatting | bytes 131072
  38.6 1.7 %copy.12 = f32[256,256]{1,0:T(8,128)} copy(f32[256,256]{1,0:T(8,128)} %get-tuple-element.5) | data formatting | bytes 524288

commit v3 on v2

--- a/solution.py
+++ b/solution.py
@@ -39,20 +39,28 @@
     )
 
 
+def flip(index, mask, count):
+    total, bit = 0, 1
+    while bit < count:
+        total = total + lax.rem(index // bit + mask // bit, 2) * bit
+        bit *= 2
+    return total
+
+
 def kernel(
     nblk, nrep, scale,
     rows_hbm, counts_hbm, grad_hbm, relu_hbm, feat_hbm, weight_hbm, tiles_hbm,
     gf_ref, gw_ref,
     rows_ref, counts_ref, grad_ref, relu_ref, feat_ref, weight_ref, tiles_ref, inputs,
     pieces, turned, feat_t, away, arrived, kept, mixed, gathered, own,
-    terms, terms_low, share_in, block_sum, block_low, part_in, final,
-    gs, gr, ps, pr, rs, rr, ts, tr, bs, br, ks, kr, fs, fr,
+    terms, terms_low, share_in, block_sum, part_in, final,
+    gs, gr, ps, pr, rs, rr, ts, tr, bs, br, fs, fr,
 ):
     me_b = lax.axis_index("blk")
     me_r = lax.axis_index("rep")
     slot_count = tiles_ref.shape[2]
     rows = terms.shape[1]
-    halves = gw_ref.shape[1] // 128
+    halves = weight_hbm.shape[1] // 128
     per_half = nblk // halves
     outer = nrep // 2
     me_o, me_i = me_r // 2, lax.rem(me_r, 2)
@@ -115,24 +123,17 @@
 
         return fold(nblk // GROUP, part, jnp.zeros(own.shape, jnp.float32))
 
-    def flip(q):
-        total, bit = 0, 1
-        while bit < outer:
-            total = total + lax.rem(me_o // bit + q // bit, 2) * bit
-            bit *= 2
-        return total
-
     def pair(q):
         return remote(away.at[q], arrived.at[q], ps.at[q], pr.at[q], {"rep": me_o * 2 + 1 - me_i})
 
     def scatter(q):
-        return remote(mixed.at[q], gathered.at[q], rs.at[q], rr.at[q], {"rep": flip(q) * 2 + me_i})
+        return remote(mixed.at[q], gathered.at[q], rs.at[q], rr.at[q], {"rep": flip(me_o, q, outer) * 2 + me_i})
 
     def send_pair(step):
         q = outer - 1 - step
-        away[q] = partial(flip(q) * 2 + 1 - me_i).astype(away.dtype)
+        away[q] = partial(flip(me_o, q, outer) * 2 + 1 - me_i).astype(away.dtype)
         pair(q).start()
-        kept[q] = partial(flip(q) * 2 + me_i)
+        kept[q] = partial(flip(me_o, q, outer) * 2 + me_i)
 
     loop(0, outer, send_pair)
 
@@ -175,59 +176,30 @@
         return total + share_in[index + 1].astype(jnp.float32)
 
     block_sum[...] = fold(nblk - 1, take_share, terms[me_b])
-    part_rows = part_in.shape[1]
-    split = part_rows < rows
-    if split:
-        block_low[...] = block_sum[...].astype(block_low.dtype)
-        mine = pl.ds(pl.multiple_of(me_r * part_rows, part_rows), part_rows)
-
-        def across(e):
-            other = lax.rem(me_r + e, nrep)
-            theirs = pl.ds(pl.multiple_of(other * part_rows, part_rows), part_rows)
-            return remote(block_low.at[theirs], part_in.at[e], bs.at[e], br.at[e], {"rep": other})
-
-        def take_part(index, total):
-            across(index + 1).wait_recv()
-            return total + part_in[index + 1].astype(jnp.float32)
-
-        loop(1, nrep, lambda e: across(e).start())
-        final[me_b, mine] = fold(nrep - 1, take_part, block_sum[mine]).astype(final.dtype)
-
-        def regain(e):
-            place = final.at[me_b, mine]
-            return remote(place, place, ks.at[e], kr.at[e], {"rep": lax.rem(me_r + e, nrep)})
-
-        loop(1, nrep, lambda e: regain(e).start())
-        loop(1, nrep, lambda e: regain(e).wait_recv())
-    else:
-        part_in[me_r] = block_sum[...].astype(part_in.dtype)
-
-        def across(e):
-            place = part_in.at[me_r]
-            return remote(place, place, bs.at[e], br.at[e], {"rep": lax.rem(me_r + e, nrep)})
-
-        loop(1, nrep, lambda e: across(e).start())
-        loop(1, nrep, lambda e: across(e).wait_recv())
-        final[me_b] = fold(
-            nrep, lambda r, total: total + part_in[r].astype(jnp.float32), jnp.zeros(block_sum.shape, jnp.float32)
-        ).astype(final.dtype)
+    part_in[me_r] = block_sum[...].astype(part_in.dtype)
+
+    def across(e):
+        place = part_in.at[me_r]
+        return remote(place, place, bs.at[e], br.at[e], {"rep": lax.rem(me_r + e, nrep)})
+
+    loop(1, nrep, lambda e: across(e).start())
+    loop(1, nrep, lambda e: across(e).wait_recv())
+    final[me_b] = fold(
+        nrep, lambda r, total: total + part_in[r].astype(jnp.float32), jnp.zeros(block_sum.shape, jnp.float32)
+    ).astype(final.dtype)
 
     def spread(d):
         return remote(final.at[me_b], final.at[me_b], fs.at[d], fr.at[d], {"blk": lax.rem(me_b + d, nblk)})
 
     loop(1, nblk, lambda d: spread(d).start())
     loop(1, nblk, lambda d: spread(d).wait_recv())
-    for p in range(nblk):
-        half, at = p // per_half, (p % per_half) * rows
-        gw_ref[at:at + rows, half * 128:half * 128 + 128] = final[p].astype(jnp.float32)
+    gw_ref[...] = final[...]
 
     loop(1, nblk, lambda d: gather(d).wait_send())
     loop(0, outer, lambda q: pair(q).wait_send())
     loop(1, outer, lambda q: scatter(q).wait_send())
     loop(1, nblk, lambda d: share(d).wait_send())
     loop(1, nrep, lambda e: across(e).wait_send())
-    if split:
-        loop(1, nrep, lambda e: regain(e).wait_send())
     loop(1, nblk, lambda d: spread(d).wait_send())
 
 
@@ -239,16 +211,15 @@
     slots = tiles.shape[2]
     rows_share = depth * width // (nblk * 128)
     outer = nrep // 2
-    rows_part = rows_share // nrep if rows_share % (16 * nrep) == 0 else rows_share
     low, high = jnp.bfloat16, jnp.float32
     vmem = pl.BlockSpec(memory_space=pltpu.VMEM)
     hbm = pl.BlockSpec(memory_space=pltpu.HBM)
     dma = pltpu.SemaphoreType.DMA
-    return pl.pallas_call(
+    grad_features, pieces = pl.pallas_call(
         functools.partial(kernel, nblk, nrep, float(rows * nrep * nblk) ** -0.5),
         out_shape=(
             jax.ShapeDtypeStruct((rows, depth), low),
-            jax.ShapeDtypeStruct((depth, width), high),
+            jax.ShapeDtypeStruct((nblk, rows_share, 128), low),
         ),
         in_specs=[hbm] * 7,
         out_specs=(vmem, vmem),
@@ -274,14 +245,12 @@
             pltpu.VMEM((nblk, rows_share, 128), low),
             pltpu.VMEM((nblk, rows_share, 128), low),
             pltpu.VMEM((rows_share, 128), high),
-            pltpu.VMEM((rows_share, 128), low),
-            pltpu.VMEM((nrep, rows_part, 128), low),
+            pltpu.VMEM((nrep, rows_share, 128), low),
             pltpu.VMEM((nblk, rows_share, 128), low),
             dma((nblk,)), dma((nblk,)),
             dma((outer,)), dma((outer,)),
             dma((outer,)), dma((outer,)),
             dma((nblk,)), dma((nblk,)),
-            dma((nrep,)), dma((nrep,)),
             dma((nrep,)), dma((nrep,)),
             dma((nblk,)), dma((nblk,)),
         ],
@@ -290,6 +259,10 @@
         ),
         cost_estimate=pl.CostEstimate(flops=10**9, bytes_accessed=10**6, transcendentals=0),
     )(jnp.swapaxes(tile_rows, 1, 2), tile_counts, grad_out, relu_bits, features, weight, tiles)
+    halves = width // 128
+    stacked = pieces.reshape(halves, depth, 128)
+    grad_weight = jnp.swapaxes(stacked, 0, 1).reshape(depth, width).astype(high)
+    return grad_features, grad_weight
 
 
 def solution(mesh):

time: 40.5 us -> 37.1 us (0.916)
  Pallas kernels: 36.5 us -> 33.7 us
  local copies, waits for them, and re-layouts: 3.14 us -> 0.63 us
  other arithmetic: 0 us -> 1.66 us
    pallas_call x1, Pallas kernels: 36.5 us -> 33.7 us  [body(): pl.pallas_call(functools.partial(kernel, nblk, nrep, float(rows * nrep *...]
    unnamed x2 -> x3, local copies, waits for them, and re-layouts: 3.14 us -> 0.63 us
    convert_element_type x0 -> x1, other arithmetic: none -> 1.66 us  [body(): grad_weight = jnp.swapaxes(stacked, 0, 1).reshape(depth, width).astype(high)]
where the time goes in v3:
time: 37.1 us; the launch traced here: 36.7 us
  Pallas kernels  33.7 us (91%)
  other arithmetic  1.66 us (4%)
  between operations  0.65 us (2%)
  local copies, waits for them, and re-layouts  0.63 us (2%)
    pallas_call x1, Pallas kernels, body(): pl.pallas_call(functools.partial(kernel, nblk, nrep, float(rows * nrep *...  33.7 us
    convert_element_type x1, other arithmetic, body(): grad_weight = jnp.swapaxes(stacked, 0, 1).reshape(depth, width).astype(high)  1.66 us

profile of v3, /device:TPU:0, one launch (start us, length us, event | category | flops | bytes accessed | tf_op | source)
XLA Modules:
  0.0 36.7 jit_solution(16098231150370074696)
XLA Ops:
  0.6 33.7 %shard_map.86 = (bf16[128,256]{1,0:T(8,128)(2,1)}, bf16[4,128,128]{2,1,0:T(8,128)(2,1)}) custom-call(s32[1,2,4]{2,1,0:T(2,128)} %bitcast.14, s32[1,4]{1,0:T(1,128)} %counts_hbm.1, bf16[128,256]{1,0:T(8,128)(2,1)} %grad_hbm.1, s32[128,256]{1,0:T(8,128)} %relu_hbm.1, bf16[128,256]{1,0:T(8,128)(2,1)} %feat_hbm.1, bf16[256,256]{1,0:T(8,128)(2,1)} %weight_hbm.1, ...), custom_call_target="tpu_custom_call" | custom-call | flops 1000000000 | bytes 1000000 | tf_op jit(solution)/shard_map/pallas_call | solution.py:218
  34.4 0.0 copy-start
  34.4 1.7 %copy_bitcast_fusion = f32[256,256]{1,0:T(8,128)} fusion(bf16[2,256,128]{2,1,0:T(8,128)(2,1)} %bitcast.13), kind=kLoop, calls=%fused_computation | loop fusion | flops 65536 | bytes 393216 | tf_op jit(solution)/shard_map/convert_element_type | solution.py:264
  36.0 0.0 copy-done
  36.0 0.6 %copy.13 = bf16[128,256]{1,0:T(8,128)(2,1)} copy(bf16[128,256]{1,0:T(8,128)(2,1)S(1)} %copy-done) | data formatting | bytes 131072
Async XLA Ops:
  34.4 1.7 %copy-start = (bf16[128,256]{1,0:T(8,128)(2,1)S(1)}, bf16[128,256]{1,0:T(8,128)(2,1)}, u32[]{:S(2)}) copy-start(bf16[128,256]{1,0:T(8,128)(2,1)} %get-tuple-element.8) | copy-start | bytes 196612
